TPU v7x, 768 devices: a whole 4x8x12 slice. The times are simulated.
768 devices in a mesh: dp: 16 (over z_hi, y), expert: 48 (over z_lo, x, core).
Axes of the slice: x: 4, y: 8, z: 12 (z_hi: 2, z_lo: 6; z = z_hi * 6 + z_lo), core: 2. Of those that a mesh axis runs over, the one named last changes fastest.
Arguments:
- tokens: bfloat16 [768, 128, 1280], P(('dp', 'expert')), may hold values from -6 to 6
- slot_param: bfloat16 [1280, 48], replicated, may hold values from -0.4472136 to 0.4472136
- out_grad: bfloat16 [768, 128, 1280], P(('dp', 'expert')), may hold values from -48 to 48
- slot_outputs: bfloat16 [768, 48, 1280], P(('dp', 'expert')), may hold values from -1.5 to 1.5
- slot_inputs: bfloat16 [384, 48, 1280], P(None, 'expert'), may hold values from -6 to 6
- w_in: bfloat16 [48, 1280, 5120], P('expert', None, 'dp'), may hold values from -0.15625 to 0.15625
- w_out: bfloat16 [48, 5120, 1280], P('expert', 'dp'), may hold values from -0.078125 to 0.078125
Outputs:
- token_grad: bfloat16 [768, 128, 1280], P(('dp', 'expert'))
- w_in_grad: bfloat16 [48, 1280, 5120], P('expert', None, 'dp')
- w_out_grad: bfloat16 [48, 5120, 1280], P('expert', 'dp')
All inputs are finite; a program needn't handle non-finite values.
Results may differ from a plain program's by a relative error of at most 0.034.
Values may be sent and summed in bfloat16 or wider, within the bound.
A program may use at most 32 MiB of HBM per device.

v0:
```python
import jax
import jax.numpy as jnp
from jax import lax
from jax.sharding import PartitionSpec as P


def gelu_pair(pre):
    normal_cdf = 0.5 * (1.0 + lax.erf(pre * 0.7071067811865476))
    normal_pdf = jnp.exp(-0.5 * pre * pre) * 0.3989422804014327
    return (pre * normal_cdf, normal_cdf + pre * normal_pdf)


def body(tokens, slot_param, out_grad, slot_outputs, slot_inputs, w_in, w_out):
    f32 = jnp.float32
    bf16 = jnp.bfloat16
    piece_tok = tokens[0]
    piece_grad = out_grad[0]
    piece_out = slot_outputs[0]
    owners = lax.axis_size("expert")
    slot_count = slot_param.shape[1]
    per_owner = slot_count // owners
    width = piece_tok.shape[1]
    pairs = owners // 2
    logits = jnp.dot(piece_tok, slot_param, preferred_element_type=f32)
    combine = jax.nn.softmax(logits, axis=1)
    comb16 = combine.astype(bf16)
    partial_value = jnp.einsum("ts,tk->sk", comb16, piece_grad, preferred_element_type=f32)
    col_max = jnp.max(logits, axis=0)
    col_sum = jnp.sum(jnp.exp(logits - col_max[None, :]), axis=0)
    part_in, max_in, sum_in = (
        lax.all_to_all(
            partial_value.reshape(owners, per_owner, width),
            "expert",
            split_axis=0,
            concat_axis=0,
            tiled=True,
        ),
        lax.all_to_all(
            col_max.reshape(owners, per_owner), "expert", split_axis=0, concat_axis=0, tiled=True
        ),
        lax.all_to_all(
            col_sum.reshape(owners, per_owner), "expert", split_axis=0, concat_axis=0, tiled=True
        ),
    )
    part_in = part_in.reshape(pairs, 2, per_owner, width)
    max_in = max_in.reshape(pairs, 2, per_owner)
    sum_in = sum_in.reshape(pairs, 2, per_owner)
    top = jnp.maximum(max_in[:, 0], max_in[:, 1])
    total = sum_in[:, 0] * jnp.exp(max_in[:, 0] - top) + sum_in[:, 1] * jnp.exp(max_in[:, 1] - top)
    norm_log = top + jnp.log(total)
    slot_grad = (part_in[:, 0] + part_in[:, 1]).astype(bf16)
    grads = lax.all_gather(slot_grad, "dp", axis=0, tiled=True)
    pre = jnp.einsum("gek,ekf->gef", slot_inputs, w_in, preferred_element_type=f32)
    act, slope = gelu_pair(pre)
    act16 = act.astype(bf16)
    hid_grad = jnp.einsum("gek,efk->gef", grads, w_out, preferred_element_type=f32)
    pre_grad = (hid_grad * slope).astype(bf16)
    w_out_grad = jnp.einsum("gef,gek->efk", act16, grads, preferred_element_type=f32).astype(bf16)
    w_in_grad = jnp.einsum(
        "gek,gef->ekf", slot_inputs, pre_grad, preferred_element_type=f32
    ).astype(bf16)
    summed = lax.psum_scatter(
        jnp.einsum("gef,ekf->gek", pre_grad, w_in, preferred_element_type=f32).astype(jnp.bfloat16),
        "dp",
        scatter_dimension=0,
        tiled=True,
    ).astype(jnp.float32)
    in_grad = summed.astype(bf16)
    own_inputs = lax.dynamic_slice_in_dim(slot_inputs, lax.axis_index("dp") * pairs, pairs, 0)
    slot_dot = jnp.sum(own_inputs.astype(f32) * in_grad.astype(f32), axis=2)
    norm_twice = jnp.broadcast_to(norm_log[:, None], (pairs, 2, per_owner)).reshape(
        owners, per_owner
    )
    dot_twice = jnp.broadcast_to(slot_dot[:, None], (pairs, 2, per_owner)).reshape(
        owners, per_owner
    )
    norm_back, dot_back = (
        lax.all_to_all(norm_twice, "expert", split_axis=0, concat_axis=0, tiled=True),
        lax.all_to_all(dot_twice, "expert", split_axis=0, concat_axis=0, tiled=True),
    )
    doubled = jnp.broadcast_to(in_grad[:, None], (pairs, 2, per_owner, width))
    grad_back = lax.all_to_all(
        doubled.reshape(owners, per_owner, width), "expert", split_axis=0, concat_axis=0, tiled=True
    )
    slot_in_grad = grad_back.reshape(slot_count, width)
    norm_back = norm_back.reshape(slot_count)
    dot_back = dot_back.reshape(slot_count)
    dispatch = jnp.exp(logits - norm_back[None, :])
    disp16 = dispatch.astype(bf16)
    disp_grad = jnp.einsum("tk,sk->ts", piece_tok, slot_in_grad, preferred_element_type=f32)
    comb_grad = jnp.einsum("tk,sk->ts", piece_grad, piece_out, preferred_element_type=f32)
    row_term = jnp.sum(combine * comb_grad, axis=1, keepdims=True)
    logit_grad = (
        combine * (comb_grad - row_term) + dispatch * (disp_grad - dot_back[None, :])
    ).astype(bf16)
    result = jnp.dot(disp16, slot_in_grad, preferred_element_type=f32)
    result = result + jnp.einsum("ts,ks->tk", logit_grad, slot_param, preferred_element_type=f32)
    return (result.astype(bf16)[None], w_in_grad, w_out_grad)


def solution(mesh):
    placed = (
        P(("dp", "expert"), None, None),
        P(),
        P(("dp", "expert"), None, None),
        P(("dp", "expert"), None, None),
        P(None, "expert", None),
        P("expert", None, "dp"),
        P("expert", "dp", None),
    )
    return jax.shard_map(
        body,
        mesh=mesh,
        in_specs=placed,
        out_specs=(
            P(("dp", "expert"), None, None),
            P("expert", None, "dp"),
            P("expert", "dp", None),
        ),
        check_vma=False,
    )
```

profile of v0, /device:TPU:1, one launch (start us, length us, event | category | flops | bytes accessed | tf_op | source)
XLA Modules:
  0.0 386.0 jit_solution(16371037802913105338)
XLA Ops:
  7.2 1.4 fusion.61
  10.8 16.4 %all-to-all-start.3 = ((f32[48,1,1280]{2,1,0:T(1,128)}), f32[48,1,1280]{2,1,0:T(1,128)S(1)}, u32[]{:S(2)}, u32[]{:S(2)}) async-start(f32[48,1,1280]{2,1,0:T(1,128)} %copy.33), calls=%async_computation.3 | async-start | bytes 491520 | tf_op jit(solution)/shard_map/all_to_all | solution.py:31
  27.9 13.5 %all-to-all-done.3 = f32[48,1,1280]{2,1,0:T(1,128)S(1)} async-done(((f32[48,1,1280]{2,1,0:T(1,128)}), f32[48,1,1280]{2,1,0:T(1,128)S(1)}, u32[]{:S(2)}, u32[]{:S(2)}) %all-to-all-start.3) | async-done | bytes 245792 | tf_op jit(solution)/shard_map/all_to_all | solution.py:31
  41.4 73.7 %all-gather = bf16[384,1,1,1280]{3,0,2,1:T(8,128)(2,1)S(1)} all-gather(bf16[24,1,1,1280]{3,0,2,1:T(8,128)(2,1)S(1)} %fusion.32), channel_id=2, replica_groups=mesh['dp'=16,'expert'=48] {'dp'}, dimensions={0}, use_global_device_ids=true | all-gather | bytes 1044480 | tf_op jit(solution)/shard_map/all_gather | solution.py:52
  116.5 1.7 fusion
  118.9 16.7 %all-to-all-start = ((f32[48,1,1]{2,1,0:T(1,128)}), f32[48,1,1]{2,1,0:T(1,128)S(1)}, u32[]{:S(2)}, u32[]{:S(2)}) async-start(f32[48,1,1]{2,1,0:T(1,128)} %copy.30), calls=%async_computation | async-start | bytes 49152 | tf_op jit(solution)/shard_map/all_to_all | solution.py:38
  135.6 2.4 multiply_reduce_fusion.1
  138.7 7.3 %all-to-all-done = f32[48,1,1]{2,1,0:T(1,128)S(1)} async-done(((f32[48,1,1]{2,1,0:T(1,128)}), f32[48,1,1]{2,1,0:T(1,128)S(1)}, u32[]{:S(2)}, u32[]{:S(2)}) %all-to-all-start) | async-done | bytes 224 | tf_op jit(solution)/shard_map/all_to_all | solution.py:38
  146.0 4.6 %all-to-all-start.1 = ((f32[48,1,1]{2,1,0:T(1,128)}), f32[48,1,1]{2,1,0:T(1,128)S(1)}, u32[]{:S(2)}, u32[]{:S(2)}) async-start(f32[48,1,1]{2,1,0:T(1,128)} %copy.31), calls=%async_computation.1 | async-start | bytes 49152 | tf_op jit(solution)/shard_map/all_to_all | solution.py:41
  151.2 9.9 %all-to-all-done.1 = f32[48,1,1]{2,1,0:T(1,128)S(1)} async-done(((f32[48,1,1]{2,1,0:T(1,128)}), f32[48,1,1]{2,1,0:T(1,128)S(1)}, u32[]{:S(2)}, u32[]{:S(2)}) %all-to-all-start.1) | async-done | bytes 224 | tf_op jit(solution)/shard_map/all_to_all | solution.py:41
  162.5 4.7 %all-to-all-start.2 = ((f32[48,1,1]{2,1,0:T(1,128)}), f32[48,1,1]{2,1,0:T(1,128)S(1)}, u32[]{:S(2)}, u32[]{:S(2)}) async-start(f32[48,1,1]{2,1,0:T(1,128)} %broadcast_in_dim.44), calls=%async_computation.2 | async-start | bytes 49152 | tf_op jit(solution)/shard_map/all_to_all | solution.py:78
  167.3 166.6 %reduce-scatter.2.cloned.1.call-done = bf16[24,1,1280]{2,0,1:T(8,128)(2,1)} async-done(((bf16[384,1,1280]{2,0,1:T(8,128)(2,1)}), bf16[24,1,1280]{2,0,1:T(8,128)(2,1)}) %reduce-scatter.2.cloned.1.call-update) | async-done | bytes 61456 | tf_op jit(solution)/shard_map/reduce_scatter | solution.py:62
  335.6 10.7 %all-to-all-start.5 = ((f32[48,1,1]{2,1,0:T(1,128)}), f32[48,1,1]{2,1,0:T(1,128)}, u32[]{:S(2)}, u32[]{:S(2)}) async-start(f32[48,1,1]{2,1,0:T(1,128)} %broadcast_in_dim.46), calls=%async_computation.6 | async-start | bytes 49152 | tf_op jit(solution)/shard_map/all_to_all | solution.py:79
  347.3 1.5 broadcast_in_dim.39
  348.9 1.3 broadcast_in_dim.45
  350.8 2.1 reduce.7
  352.9 1.6 reshape.161
  354.5 2.2 all-to-all-done.5
  356.7 8.8 %all-to-all-start.4 = ((bf16[48,2,640]{2,1,0:T(2,128)(2,1)}), bf16[48,2,640]{2,1,0:T(2,128)(2,1)S(1)}, u32[]{:S(2)}, u32[]{:S(2)}) async-start(bf16[48,2,640]{2,1,0:T(2,128)(2,1)} %reshape.161), calls=%async_computation.5 | async-start | bytes 245760 | tf_op jit(solution)/shard_map/all_to_all | solution.py:82
  365.5 2.4 fusion.1
  368.0 1.5 fusion.2
  369.5 1.2 reduce.5
  370.7 6.6 %all-to-all-done.4 = bf16[48,2,640]{2,1,0:T(2,128)(2,1)S(1)} async-done(((bf16[48,2,640]{2,1,0:T(2,128)(2,1)}), bf16[48,2,640]{2,1,0:T(2,128)(2,1)S(1)}, u32[]{:S(2)}, u32[]{:S(2)}) %all-to-all-start.4) | async-done | bytes 122912 | tf_op jit(solution)/shard_map/all_to_all | solution.py:82
  377.8 1.4 fusion.4
  (46 shorter events, 11.5 us)
Async XLA Ops:
  7.2 20.1 %copy-start = (bf16[1,1280,320]{1,2,0:T(8,128)(2,1)S(1)}, bf16[1,1280,320]{1,2,0:T(8,128)(2,1)}, u32[]{:S(2)}) copy-start(bf16[1,1280,320]{1,2,0:T(8,128)(2,1)} %param.12) | copy-start | bytes 2457604
  7.2 20.1 %copy-start.1 = (bf16[384,1,1280]{2,0,1:T(8,128)(2,1)S(1)}, bf16[384,1,1280]{2,0,1:T(8,128)(2,1)}, u32[]{:S(2)}) copy-start(bf16[384,1,1280]{2,0,1:T(8,128)(2,1)} %param.11) | copy-start | bytes 2949124
  10.8 30.6 %all-to-all-start.3 = ((f32[48,1,1280]{2,1,0:T(1,128)}), f32[48,1,1280]{2,1,0:T(1,128)S(1)}, u32[]{:S(2)}, u32[]{:S(2)}) async-start(f32[48,1,1280]{2,1,0:T(1,128)} %copy.33), calls=%async_computation.3 | async-start | bytes 491520 | tf_op jit(solution)/shard_map/all_to_all | solution.py:31
  27.2 306.7 %reduce-scatter.2.cloned.1.call-start = ((), (), s32[]{:S(2)}) async-start(), calls=%async_computation.7 | async-start | bytes 1044480 | tf_op jit(solution)/shard_map/reduce_scatter | solution.py:62
  41.4 73.8 %copy-start.9 = (bf16[1,320,1280]{2,1,0:T(8,128)(2,1)S(1)}, bf16[1,320,1280]{2,1,0:T(8,128)(2,1)}, u32[]{:S(2)}) copy-start(bf16[1,320,1280]{2,1,0:T(8,128)(2,1)} %param.13) | copy-start | bytes 2457604
  115.8 0.7 copy-start.3
  118.2 17.4 %copy-start.5 = (bf16[1,48,1280]{2,1,0:T(8,128)(2,1)S(1)}, bf16[1,48,1280]{2,1,0:T(8,128)(2,1)}, u32[]{:S(2)}) copy-start(bf16[1,48,1280]{2,1,0:T(8,128)(2,1)} %param.10) | copy-start | bytes 368644
  118.9 27.1 %all-to-all-start = ((f32[48,1,1]{2,1,0:T(1,128)}), f32[48,1,1]{2,1,0:T(1,128)S(1)}, u32[]{:S(2)}, u32[]{:S(2)}) async-start(f32[48,1,1]{2,1,0:T(1,128)} %copy.30), calls=%async_computation | async-start | bytes 49152 | tf_op jit(solution)/shard_map/all_to_all | solution.py:38
  146.0 15.0 %all-to-all-start.1 = ((f32[48,1,1]{2,1,0:T(1,128)}), f32[48,1,1]{2,1,0:T(1,128)S(1)}, u32[]{:S(2)}, u32[]{:S(2)}) async-start(f32[48,1,1]{2,1,0:T(1,128)} %copy.31), calls=%async_computation.1 | async-start | bytes 49152 | tf_op jit(solution)/shard_map/all_to_all | solution.py:41
  162.5 173.1 %all-to-all-start.2 = ((f32[48,1,1]{2,1,0:T(1,128)}), f32[48,1,1]{2,1,0:T(1,128)S(1)}, u32[]{:S(2)}, u32[]{:S(2)}) async-start(f32[48,1,1]{2,1,0:T(1,128)} %broadcast_in_dim.44), calls=%async_computation.2 | async-start | bytes 49152 | tf_op jit(solution)/shard_map/all_to_all | solution.py:78
  335.6 21.1 %all-to-all-start.5 = ((f32[48,1,1]{2,1,0:T(1,128)}), f32[48,1,1]{2,1,0:T(1,128)}, u32[]{:S(2)}, u32[]{:S(2)}) async-start(f32[48,1,1]{2,1,0:T(1,128)} %broadcast_in_dim.46), calls=%async_computation.6 | async-start | bytes 49152 | tf_op jit(solution)/shard_map/all_to_all | solution.py:79
  356.7 20.6 %all-to-all-start.4 = ((bf16[48,2,640]{2,1,0:T(2,128)(2,1)}), bf16[48,2,640]{2,1,0:T(2,128)(2,1)S(1)}, u32[]{:S(2)}, u32[]{:S(2)}) async-start(bf16[48,2,640]{2,1,0:T(2,128)(2,1)} %reshape.161), calls=%async_computation.5 | async-start | bytes 245760 | tf_op jit(solution)/shard_map/all_to_all | solution.py:82
  368.0 9.5 %copy-start.7 = (f32[48]{0:T(128)S(1)}, f32[48]{0:T(128)}, u32[]{:S(2)}) copy-start(f32[48]{0:T(128)} %reduce.4) | copy-start | bytes 580
  369.4 8.3 %copy-start.2 = (bf16[1,128,1280]{2,1,0:T(8,128)(2,1)S(1)}, bf16[1,128,1280]{2,1,0:T(8,128)(2,1)}, u32[]{:S(2)}) copy-start(bf16[1,128,1280]{2,1,0:T(8,128)(2,1)} %param.7) | copy-start | bytes 983044
  369.4 8.4 %copy-start.4 = (bf16[1280,48]{0,1:T(8,128)(2,1)S(1)}, bf16[1280,48]{0,1:T(8,128)(2,1)}, u32[]{:S(2)}) copy-start(bf16[1280,48]{0,1:T(8,128)(2,1)} %param.8) | copy-start | bytes 368644
  369.4 8.4 %copy-start.6 = (f32[128,48]{0,1:T(8,128)S(1)}, f32[128,48]{0,1:T(8,128)}, u32[]{:S(2)}) copy-start(f32[128,48]{0,1:T(8,128)} %get-tuple-element.11) | copy-start | bytes 73732
  369.5 8.4 %copy-start.8 = (f32[128]{0:T(128)S(1)}, f32[128]{0:T(128)}, u32[]{:S(2)}) copy-start(f32[128]{0:T(128)} %get-tuple-element.3) | copy-start | bytes 1540
Sparse Core Ops, SparseCore 0:
  118.3 215.5 reduce-scatter.1
where the time goes:
time: 387 us; the launch traced here: 386 us
  waiting for transfers between devices  206 us (53%)
  blocking collectives  73.7 us (19%)
  starting transfers between devices  62 us (16%)
  between operations  14.3 us (4%)
  matrix products  13.4 us (3%)
  local copies, waits for them, and re-layouts  9.96 us (3%)
  other arithmetic  6.47 us (2%)
    reduce_scatter x1, waiting for transfers between devices, body(): lax.psum_scatter(jnp.einsum('gef,ekf->gek', pre_grad, w_in, preferred_ele...  167 us
    all_gather x1, blocking collectives, body(): grads = lax.all_gather(slot_grad, 'dp', axis=0, tiled=True)  73.7 us
    all_to_all x1, starting transfers between devices, body(): lax.all_to_all(col_max.reshape(owners, per_owner), 'expert', split_axis=0...  16.7 us
    all_to_all x1, starting transfers between devices, body(): lax.all_to_all(partial_value.reshape(owners, per_owner, width), 'expert',...  16.4 us
    all_to_all x1, waiting for transfers between devices, body(): lax.all_to_all(partial_value.reshape(owners, per_owner, width), 'expert',...  13.5 us
    all_to_all x1, starting transfers between devices, body(): lax.all_to_all(dot_twice, 'expert', split_axis=0, concat_axis=0, tiled=True)  10.7 us
    all_to_all x1, waiting for transfers between devices, body(): lax.all_to_all(col_sum.reshape(owners, per_owner), 'expert', split_axis=0...  9.86 us
    all_to_all x1, starting transfers between devices, body(): lax.all_to_all(doubled.reshape(owners, per_owner, width), 'expert', split...  8.82 us
  transfers between devices with their start and end apart: 7, of which 6 were waited for; matrix products, arithmetic and copies ran while one was open for 6% of the time, Pallas kernels for 0%

commit v1 on v0

v1 whole, which is shorter than its diff:
```python
import jax
import jax.numpy as jnp
from jax import lax
from jax.experimental import pallas as pl
from jax.experimental.pallas import tpu as pltpu
from jax.sharding import PartitionSpec as P

F32 = jnp.float32
BF16 = jnp.bfloat16
MESH = pl.DeviceIdType.MESH

RING = 8
HALVES = 2
CHIPS = 24
BLOCK = HALVES * CHIPS
PIECE = 16
LANES = 128


def matmul(a, b):
    return lax.dot_general(a, b, (((1,), (0,)), ((), ())), preferred_element_type=F32)


def matmul_t(a, b):
    return lax.dot_general(a, b, (((1,), (1,)), ((), ())), preferred_element_type=F32)


def gelu_pair(pre):
    normal_cdf = 0.5 * (1.0 + lax.erf(pre * 0.7071067811865476))
    normal_pdf = jnp.exp(-0.5 * pre * pre) * 0.3989422804014327
    return pre * normal_cdf, normal_cdf + pre * normal_pdf


def kernel(
    tok_in, param_in, ograd_in, sout_in, x_in, win_in, wout_in,
    tok_grad, win_grad, wout_grad,
    tok, param, ograd, sout, x, win, wout,
    param_p, xp, slope, act_t, grads, pgs, pg_t, sums,
    part, pair_part, lse_own, lse_pair, disp, base,
    tiles, out_a, in_a, out_b, in_b, back,
    rs_out_r, rs_out_l, rs_in_r, rs_in_l,
    local_sem, pair_send, pair_recv, all_send, all_recv, all_self,
    ag_send, ag_recv, rs_send, rs_recv,
):
    width = tok.shape[1]
    half = width // 2
    cuts = width // LANES
    d = lax.axis_index("dp")
    e = lax.axis_index("expert")
    zh, y = d // RING, d % RING
    chip, core = e // 2, e % 2
    me = zh * CHIPS + chip
    other = (d, e + 1 - 2 * core)
    right = (zh * RING + (y + 1) % RING, e)
    left = (zh * RING + (y + RING - 1) % RING, e)

    def peer(n):
        t = (me + n) % BLOCK
        return t, t % CHIPS, ((t // CHIPS) * RING + y, 2 * (t % CHIPS) + core)

    loads = [
        pltpu.make_async_copy(src, dst, local_sem.at[i])
        for i, (src, dst) in enumerate(
            [(tok_in, tok), (param_in, param), (ograd_in, ograd), (x_in, x),
             (win_in, win), (sout_in, sout), (wout_in, wout)]
        )
    ]
    for load in loads:
        load.start()

    barrier = pltpu.get_barrier_semaphore()
    for device in (other, left, right):
        pl.semaphore_signal(barrier, inc=1, device_id=device, device_id_type=MESH)

    @pl.loop(1, BLOCK)
    def _(n):
        _, _, device = peer(n)
        pl.semaphore_signal(barrier, inc=1, device_id=device, device_id_type=MESH)

    row = lax.broadcasted_iota(jnp.int32, (BLOCK, BLOCK), 0)
    col = lax.broadcasted_iota(jnp.int32, (BLOCK, BLOCK), 1)
    wanted = jnp.where(row < CHIPS, 2 * row, 2 * (row - CHIPS) + 1)
    perm = jnp.where(col == wanted, 1.0, 0.0).astype(BF16)
    loads[0].wait()
    loads[1].wait()
    param_p[...] = matmul(perm, param[...]).astype(BF16)
    logits = matmul_t(param_p[...], tok[...])
    ex = jnp.exp(logits - jnp.max(logits, axis=0, keepdims=True))
    combine = ex / jnp.sum(ex, axis=0, keepdims=True)
    loads[2].wait()
    part[...] = matmul(combine.astype(BF16), ograd[...])
    col_max = jnp.max(logits, axis=1, keepdims=True)
    col_sum = jnp.sum(jnp.exp(logits - col_max), axis=1, keepdims=True)
    lse_own[...] = jnp.broadcast_to(col_max + jnp.log(col_sum), lse_own.shape)

    pl.semaphore_wait(barrier, BLOCK - 1 + 3)
    mine = pl.ds(pl.multiple_of(CHIPS * core, 8), CHIPS)
    theirs = pl.ds(pl.multiple_of(CHIPS * (1 - core), 8), CHIPS)
    send_part = pltpu.make_async_remote_copy(
        part.at[theirs], pair_part, pair_send.at[0], pair_recv.at[0], device_id=other, device_id_type=MESH
    )
    send_part.start()
    send_lse = pltpu.make_async_remote_copy(
        lse_own, lse_pair, pair_send.at[1], pair_recv.at[1], device_id=other, device_id_type=MESH
    )
    send_lse.start()

    tiles[...] = jnp.zeros_like(tiles)
    send_part.wait_recv()
    slot_sum = (part[mine, :] + pair_part[...]).astype(BF16).astype(F32)
    for i in range(cuts):
        tiles[pl.ds(i, CHIPS, stride=PIECE), :] = slot_sum[:, i * LANES:(i + 1) * LANES]
    out_a[...] = tiles[pl.ds(0, CHIPS * PIECE), :].astype(BF16)

    def piece(ref, i):
        return ref.at[pl.ds(pl.multiple_of(i * PIECE, PIECE), PIECE)]

    all_but_one = pl.ds(0, (BLOCK - 1) * PIECE)

    @pl.loop(1, BLOCK)
    def _(n):
        _, owner, device = peer(n)
        pltpu.make_async_remote_copy(
            piece(out_a, owner), piece(in_a, me), all_send.at[0], all_recv.at[0],
            device_id=device, device_id_type=MESH,
        ).start()

    self_a = pltpu.make_async_copy(piece(out_a, chip), piece(in_a, me), all_self.at[0])
    self_a.start()

    loads[3].wait()
    for b in range(RING):
        lo = x[b * CHIPS:(b + 1) * CHIPS, :]
        hi = x[(RING + b) * CHIPS:(RING + b + 1) * CHIPS, :]
        xp[b * BLOCK:(b + 1) * BLOCK, :] = jnp.concatenate([lo, hi], axis=0)
    loads[4].wait()
    for i in range(xp.shape[0] // LANES):
        rows = slice(i * LANES, (i + 1) * LANES)
        act, rise = gelu_pair(matmul_t(xp[rows, :], win[...]))
        slope[rows, :] = rise
        act_t[:, rows] = act.T.astype(BF16)
    loads[5].wait()
    comb_grad = matmul_t(matmul(perm, sout[...]).astype(BF16), ograd[...])
    base[...] = combine * (comb_grad - jnp.sum(combine * comb_grad, axis=0, keepdims=True))
    send_lse.wait_recv()
    lse_a, lse_b = lse_own[...], lse_pair[...]
    top = jnp.maximum(lse_a, lse_b)
    lse = top + jnp.log(jnp.exp(lse_a - top) + jnp.exp(lse_b - top))
    disp[...] = jnp.exp(logits - lse)

    def rows_of(b):
        return pl.ds(pl.multiple_of(b * BLOCK, PIECE), BLOCK)

    pltpu.make_async_copy(in_a.at[all_but_one], in_a.at[all_but_one], all_recv.at[0]).wait()
    self_a.wait()
    tiles[...] = in_a[...].astype(F32)
    for i in range(cuts):
        grads[rows_of(y), i * LANES:(i + 1) * LANES] = tiles[pl.ds(i, BLOCK, stride=PIECE), :].astype(BF16)
    loads[6].wait()

    def work(blocks):
        g = [grads[rows_of(b), :] for b in blocks]
        s = [slope[rows_of(b), :] for b in blocks]
        g = g[0] if len(g) == 1 else jnp.concatenate(g, axis=0)
        s = s[0] if len(s) == 1 else jnp.concatenate(s, axis=0)
        pg = (matmul_t(g, wout[...]) * s).astype(BF16)
        total = matmul(pg, win[...])
        for i, b in enumerate(blocks):
            pgs[rows_of(b), :] = pg[i * BLOCK:(i + 1) * BLOCK, :]
            sums[rows_of(b), :] = total[i * BLOCK:(i + 1) * BLOCK, :]

    def at(offset):
        return (y + offset + RING) % RING

    lanes_r, lanes_l = pl.ds(0, half), pl.ds(half, half)
    ag = []
    for s in range(4):
        to_r = grads.at[rows_of(at(-s))]
        to_l = grads.at[rows_of(at(s))]
        if s == 3:
            to_r = grads.at[rows_of(at(-s)), lanes_r]
            to_l = grads.at[rows_of(at(s)), lanes_l]
        pair = [
            pltpu.make_async_remote_copy(
                ref, ref, ag_send.at[s, i], ag_recv.at[s, i], device_id=device, device_id_type=MESH
            )
            for i, (ref, device) in enumerate(((to_r, right), (to_l, left)))
        ]
        for copy in pair:
            copy.start()
        work([at(0)] if s == 0 else [at(-s), at(s)])
        for copy in pair:
            copy.wait_recv()
        ag += pair
    work([at(4)])

    rs = []
    chunk = 2 * LANES

    def weight_out():
        for i in range(width // chunk):
            lanes = slice(i * chunk, (i + 1) * chunk)
            wout_grad[:, lanes] = matmul(act_t[...], grads[:, lanes]).astype(BF16)

    def transpose_pg():
        for i in range(pgs.shape[0] // LANES):
            rows = slice(i * LANES, (i + 1) * LANES)
            pg_t[:, rows] = pgs[rows, :].astype(F32).T.astype(BF16)

    def weight_in():
        for i in range(width // chunk):
            lanes = slice(i * chunk, (i + 1) * chunk)
            win_grad[:, lanes] = matmul(pg_t[...], xp[:, lanes]).astype(BF16)

    beside = (weight_out, transpose_pg, weight_in, lambda: None)
    for s in range(4):
        dest_r, dest_l = rows_of(at(4 - s)), rows_of(at(s - 4))
        if s == 0:
            rs_out_r[0] = sums[dest_r, :].astype(BF16)
            moves = (
                (rs_out_r.at[0, :, lanes_r], rs_in_r.at[0, :, lanes_r], right),
                (rs_out_r.at[0, :, lanes_l], rs_in_l.at[0, :, lanes_l], left),
            )
        else:
            if s == 1:
                rs_out_r[s, :, :half] = (sums[dest_r, :half] + rs_in_r[0, :, :half].astype(F32)).astype(BF16)
                rs_out_r[s, :, half:] = sums[dest_r, half:].astype(BF16)
                rs_out_l[s, :, :half] = sums[dest_l, :half].astype(BF16)
                rs_out_l[s, :, half:] = (sums[dest_l, half:] + rs_in_l[0, :, half:].astype(F32)).astype(BF16)
            else:
                rs_out_r[s] = (sums[dest_r, :] + rs_in_r[s - 1].astype(F32)).astype(BF16)
                rs_out_l[s] = (sums[dest_l, :] + rs_in_l[s - 1].astype(F32)).astype(BF16)
            moves = (
                (rs_out_r.at[s], rs_in_r.at[s], right),
                (rs_out_l.at[s], rs_in_l.at[s], left),
            )
        pair = [
            pltpu.make_async_remote_copy(
                src, dst, rs_send.at[s, i], rs_recv.at[s, i], device_id=device, device_id_type=MESH
            )
            for i, (src, dst, device) in enumerate(moves)
        ]
        for copy in pair:
            copy.start()
        beside[s]()
        for copy in pair:
            copy.wait_recv()
        rs += pair

    total = (sums[rows_of(y), :] + rs_in_r[3].astype(F32) + rs_in_l[3].astype(F32)).astype(BF16).astype(F32)
    dot = jnp.sum(xp[rows_of(y), :].astype(F32) * total, axis=1, keepdims=True)
    dot_hi = dot.astype(BF16).astype(F32)
    for i in range(cuts):
        tiles[pl.ds(i, BLOCK, stride=PIECE), :] = total[:, i * LANES:(i + 1) * LANES]
    tiles[pl.ds(cuts, BLOCK, stride=PIECE), :] = jnp.broadcast_to(dot_hi, (BLOCK, LANES))
    tiles[pl.ds(cuts + 1, BLOCK, stride=PIECE), :] = jnp.broadcast_to(dot - dot_hi, (BLOCK, LANES))
    out_b[...] = tiles[...].astype(BF16)

    @pl.loop(1, BLOCK)
    def _(n):
        t, _, device = peer(n)
        pltpu.make_async_remote_copy(
            piece(out_b, t), piece(in_b, me), all_send.at[1], all_recv.at[1],
            device_id=device, device_id_type=MESH,
        ).start()

    self_b = pltpu.make_async_copy(piece(out_b, me), piece(in_b, me), all_self.at[1])
    self_b.start()
    pltpu.make_async_copy(in_b.at[all_but_one], in_b.at[all_but_one], all_recv.at[1]).wait()
    self_b.wait()

    tiles[...] = in_b[...].astype(F32)

    def both(i):
        v = tiles[pl.ds(i, BLOCK, stride=PIECE), :]
        return v[:CHIPS, :] + v[CHIPS:, :]

    for i in range(cuts):
        back[mine, i * LANES:(i + 1) * LANES] = both(i)
    back[mine, width:width + LANES] = both(cuts) + both(cuts + 1)
    send_back = pltpu.make_async_remote_copy(
        back.at[mine], back.at[mine], pair_send.at[2], pair_recv.at[2], device_id=other, device_id_type=MESH
    )
    send_back.start()
    send_back.wait_recv()

    in_grad = back[:, :width].astype(BF16)
    disp_grad = matmul_t(in_grad, tok[...])
    logit_grad = base[...] + disp[...] * (disp_grad - back[:, width:width + LANES])
    left_t = jnp.concatenate([disp[...], logit_grad], axis=0).T.astype(BF16)
    tok_grad[...] = matmul(left_t, jnp.concatenate([in_grad, param_p[...]], axis=0)).astype(BF16)

    send_part.wait_send()
    send_lse.wait_send()
    send_back.wait_send()
    for i in range(2):
        pltpu.make_async_copy(in_b.at[all_but_one], in_b.at[all_but_one], all_send.at[i]).wait()
    for copy in ag + rs:
        copy.wait_send()


def body(tokens, slot_param, out_grad, slot_outputs, slot_inputs, w_in, w_out):
    tok, ograd, sout = tokens[0], out_grad[0], slot_outputs[0]
    x = slot_inputs[:, 0]
    param = slot_param.T
    win, wout = w_in[0].T, w_out[0]
    images, width = x.shape
    hidden = wout.shape[0]
    slots = param.shape[0]
    tokens_here = tok.shape[0]
    vm = pltpu.VMEM
    dma = pltpu.SemaphoreType.DMA
    any_space = pl.BlockSpec(memory_space=pl.ANY)
    vmem = pl.BlockSpec(memory_space=pltpu.VMEM)
    tok_grad, win_grad, wout_grad = pl.pallas_call(
        kernel,
        out_shape=(
            jax.ShapeDtypeStruct((tokens_here, width), BF16),
            jax.ShapeDtypeStruct((hidden, width), BF16),
            jax.ShapeDtypeStruct((hidden, width), BF16),
        ),
        in_specs=[any_space] * 7,
        out_specs=(vmem, vmem, vmem),
        scratch_shapes=[
            vm((tokens_here, width), BF16), vm((slots, width), BF16), vm((tokens_here, width), BF16),
            vm((slots, width), BF16), vm((images, width), BF16), vm((hidden, width), BF16),
            vm((hidden, width), BF16),
            vm((slots, width), BF16), vm((images, width), BF16), vm((images, hidden), F32),
            vm((hidden, images), BF16), vm((images, width), BF16), vm((images, hidden), BF16),
            vm((hidden, images), BF16), vm((images, width), F32),
            vm((slots, width), F32), vm((CHIPS, width), F32), vm((slots, LANES), F32),
            vm((slots, LANES), F32), vm((slots, LANES), F32), vm((slots, LANES), F32),
            vm((BLOCK * PIECE, LANES), F32), vm((CHIPS * PIECE, LANES), BF16),
            vm((BLOCK * PIECE, LANES), BF16), vm((BLOCK * PIECE, LANES), BF16),
            vm((BLOCK * PIECE, LANES), BF16), vm((slots, width + LANES), F32),
            vm((4, BLOCK, width), BF16), vm((4, BLOCK, width), BF16),
            vm((4, BLOCK, width), BF16), vm((4, BLOCK, width), BF16),
            dma((7,)), dma((3,)), dma((3,)), dma((2,)), dma((2,)), dma((2,)),
            dma((4, 2)), dma((4, 2)), dma((4, 2)), dma((4, 2)),
        ],
        compiler_params=pltpu.CompilerParams(
            collective_id=0, has_side_effects=True, vmem_limit_bytes=40 * 1024 * 1024
        ),
    )(tok, param, ograd, sout, x, win, wout)
    return tok_grad[None], win_grad.T[None], wout_grad[None]


def solution(mesh):
    placed = (
        P(("dp", "expert"), None, None),
        P(),
        P(("dp", "expert"), None, None),
        P(("dp", "expert"), None, None),
        P(None, "expert", None),
        P("expert", None, "dp"),
        P("expert", "dp", None),
    )
    return jax.shard_map(
        body,
        mesh=mesh,
        in_specs=placed,
        out_specs=(
            P(("dp", "expert"), None, None),
            P("expert", None, "dp"),
            P("expert", "dp", None),
        ),
        check_vma=False,
    )
```

time: 387 us -> 96.3 us (0.25)
  waiting for transfers between devices: 206 us -> 0 us
  Pallas kernels: 0 us -> 85.5 us
  blocking collectives: 73.7 us -> 0 us
  starting transfers between devices: 62 us -> 0 us
  between operations: 14.3 us -> 0.66 us
  matrix products: 13.4 us -> 0 us
  other arithmetic: 6.47 us -> 0 us
    reduce_scatter x1 -> x0, waiting for transfers between devices: 167 us -> none  [body(): lax.psum_scatter(jnp.einsum('gef,ekf->gek', pre_grad, w_in, preferred_ele...]
    pallas_call x0 -> x1, Pallas kernels: none -> 85.5 us  [body(): pl.pallas_call(kernel, out_shape=(jax.ShapeDtypeStruct((tokens_here, widt...]
    all_gather x1 -> x0, blocking collectives: 73.7 us -> none  [body(): grads = lax.all_gather(slot_grad, 'dp', axis=0, tiled=True)]
    all_to_all x6 -> x0, starting transfers between devices: 62 us -> none  [the longest x1 16.7 us: body(): lax.all_to_all(col_max.reshape(owners, per_owner), 'expert', split_axis=0...]
    all_to_all x6 -> x0, waiting for transfers between devices: 39.5 us -> none  [the longest x1 13.5 us: body(): lax.all_to_all(partial_value.reshape(owners, per_owner, width), 'expert',...]
    dot_general x10 -> x0, matrix products: 13.4 us -> none  [the longest x1 2.43 us: body(): jnp.einsum('gek,gef->ekf', slot_inputs, pre_grad, preferred_element_type=...]
    unnamed x22 -> x17, local copies, waits for them, and re-layouts: 2.39 us -> 9.74 us
    broadcast_in_dim x7 -> x0, local copies, waits for them, and re-layouts: 5.01 us -> none  [the longest x3 3.46 us: body(): doubled = jnp.broadcast_to(in_grad[:, None], (pairs, 2, per_owner, width))]
  transfers between devices with their start and end apart: 7 -> 0, of which waited for: 6 -> 0; matrix products, arithmetic and copies ran while one was open for 6% -> 0% of each run, Pallas kernels for 0% -> 0%
where the time goes in v1:
time: 96.3 us; the launch traced here: 95.9 us
  Pallas kernels  85.5 us (89%)
  local copies, waits for them, and re-layouts  9.74 us (10%)
    pallas_call x1, Pallas kernels, body(): pl.pallas_call(kernel, out_shape=(jax.ShapeDtypeStruct((tokens_here, widt...  85.5 us
    unnamed x17, local copies, waits for them, and re-layouts  9.74 us

profile of v1, /device:TPU:1, one launch (start us, length us, event | category | flops | bytes accessed | tf_op | source)
XLA Modules:
  0.0 95.9 jit_solution(854942933503273203)
XLA Ops:
  0.6 0.0 copy-start
  0.6 1.2 %copy-done = bf16[384,1,1280]{2,0,1:T(8,128)(2,1)S(1)} copy-done((bf16[384,1,1280]{2,0,1:T(8,128)(2,1)S(1)}, bf16[384,1,1280]{2,0,1:T(8,128)(2,1)}, u32[]{:S(2)}) %copy-start) | copy-done | bytes 983064
  1.8 0.0 copy-start.1
  1.8 1.1 %copy-done.1 = bf16[1,1280,320]{1,2,0:T(8,128)(2,1)S(1)} copy-done((bf16[1,1280,320]{1,2,0:T(8,128)(2,1)S(1)}, bf16[1,1280,320]{1,2,0:T(8,128)(2,1)}, u32[]{:S(2)}) %copy-start.1) | copy-done | bytes 819224
  3.0 0.0 copy-start.2
  3.0 1.1 %copy-done.2 = bf16[1,320,1280]{2,1,0:T(8,128)(2,1)S(1)} copy-done((bf16[1,320,1280]{2,1,0:T(8,128)(2,1)S(1)}, bf16[1,320,1280]{2,1,0:T(8,128)(2,1)}, u32[]{:S(2)}) %copy-start.2) | copy-done | bytes 819224
  4.1 0.0 copy-start.3
  4.1 1.0 %copy-done.3 = bf16[1,128,1280]{2,1,0:T(8,128)(2,1)S(1)} copy-done((bf16[1,128,1280]{2,1,0:T(8,128)(2,1)S(1)}, bf16[1,128,1280]{2,1,0:T(8,128)(2,1)}, u32[]{:S(2)}) %copy-start.3) | copy-done | bytes 327704
  5.1 0.0 copy-start.4
  5.1 1.0 %copy-done.4 = bf16[1,128,1280]{2,1,0:T(8,128)(2,1)S(1)} copy-done((bf16[1,128,1280]{2,1,0:T(8,128)(2,1)S(1)}, bf16[1,128,1280]{2,1,0:T(8,128)(2,1)}, u32[]{:S(2)}) %copy-start.4) | copy-done | bytes 327704
  6.1 0.0 copy-start.5
  6.1 0.9 copy-done.5
  7.0 0.0 copy-start.6
  7.0 0.9 copy-done.6
  7.9 85.5 %shard_map.94 = (bf16[128,1280]{1,0:T(8,128)(2,1)S(1)}, bf16[320,1280]{1,0:T(8,128)(2,1)S(1)}, bf16[320,1280]{1,0:T(8,128)(2,1)S(1)}) custom-call(bf16[128,1280]{1,0:T(8,128)(2,1)S(1)} %bitcast.19, bf16[48,1280]{1,0:T(8,128)(2,1)S(1)} %bitcast.22, bf16[128,1280]{1,0:T(8,128)(2,1)S(1)} %bitcast.20, bf16[48,1280]{1,0:T(8,128)(2,1)S(1)} %bitcast.23, ...), custom_call_target="tpu_custom_call" | custom-call | tf_op jit(solution)/shard_map/pallas_call | solution.py:315
  93.4 0.7 copy.13
  94.1 0.9 copy.14
  95.0 0.9 copy.15
Async XLA Ops:
  0.6 1.2 %copy-start = (bf16[384,1,1280]{2,0,1:T(8,128)(2,1)S(1)}, bf16[384,1,1280]{2,0,1:T(8,128)(2,1)}, u32[]{:S(2)}) copy-start(bf16[384,1,1280]{2,0,1:T(8,128)(2,1)} %param.11) | copy-start | bytes 2949124
  1.8 1.1 %copy-start.1 = (bf16[1,1280,320]{1,2,0:T(8,128)(2,1)S(1)}, bf16[1,1280,320]{1,2,0:T(8,128)(2,1)}, u32[]{:S(2)}) copy-start(bf16[1,1280,320]{1,2,0:T(8,128)(2,1)} %param.12) | copy-start | bytes 2457604
  3.0 1.1 %copy-start.2 = (bf16[1,320,1280]{2,1,0:T(8,128)(2,1)S(1)}, bf16[1,320,1280]{2,1,0:T(8,128)(2,1)}, u32[]{:S(2)}) copy-start(bf16[1,320,1280]{2,1,0:T(8,128)(2,1)} %param.13) | copy-start | bytes 2457604
  4.1 1.0 %copy-start.3 = (bf16[1,128,1280]{2,1,0:T(8,128)(2,1)S(1)}, bf16[1,128,1280]{2,1,0:T(8,128)(2,1)}, u32[]{:S(2)}) copy-start(bf16[1,128,1280]{2,1,0:T(8,128)(2,1)} %param.7) | copy-start | bytes 983044
  5.1 1.0 %copy-start.4 = (bf16[1,128,1280]{2,1,0:T(8,128)(2,1)S(1)}, bf16[1,128,1280]{2,1,0:T(8,128)(2,1)}, u32[]{:S(2)}) copy-start(bf16[1,128,1280]{2,1,0:T(8,128)(2,1)} %param.9) | copy-start | bytes 983044
  6.1 0.9 copy-start.5
  7.0 0.9 copy-start.6

commit v2 on v1

v2 whole, which is shorter than its diff:
```python
import jax
import jax.numpy as jnp
from jax import lax
from jax.experimental import pallas as pl
from jax.experimental.pallas import tpu as pltpu
from jax.sharding import PartitionSpec as P

F32 = jnp.float32
BF16 = jnp.bfloat16
MESH = pl.DeviceIdType.MESH

RING = 8
HALVES = 2
CHIPS = 24
BLOCK = HALVES * CHIPS
PIECE = 16
LANES = 128
PARTS = ((0, 384), (384, 256), (640, 384), (1024, 256))
OPPOSITE = ((0, 1), (2, 3))


def matmul(a, b):
    return lax.dot_general(a, b, (((1,), (0,)), ((), ())), preferred_element_type=F32)


def matmul_t(a, b):
    return lax.dot_general(a, b, (((1,), (1,)), ((), ())), preferred_element_type=F32)


def gelu_pair(pre):
    normal_cdf = 0.5 * (1.0 + lax.erf(pre * 0.7071067811865476))
    normal_pdf = jnp.exp(-0.5 * pre * pre) * 0.3989422804014327
    return pre * normal_cdf, normal_cdf + pre * normal_pdf


def kernel(
    tok_in, param_in, ograd_in, sout_in, x_in, win_in, wout_in,
    win_out, wout_out, tok, param_p, base, disp, back,
    param, ograd, sout, x, win, wout,
    xp, slope, act_t, grads, pgs, pg_t, sums,
    part, pair_part, lse_own, lse_pair,
    tiles, out_a, in_a, out_b, in_b,
    rs_out, rs_in, out_part,
    local_sem, pair_send, pair_recv, all_send, all_recv, all_self,
    ag_send, ag_recv, rs_send, rs_recv,
):
    width = tok.shape[1]
    cuts = width // LANES
    d = lax.axis_index("dp")
    e = lax.axis_index("expert")
    zh, y = d // RING, d % RING
    chip, core = e // 2, e % 2
    me = zh * CHIPS + chip
    other = (d, e + 1 - 2 * core)
    right = (zh * RING + (y + 1) % RING, e)
    left = (zh * RING + (y + RING - 1) % RING, e)

    def peer(n):
        t = (me + CHIPS + n) % BLOCK
        return t, t % CHIPS, ((t // CHIPS) * RING + y, 2 * (t % CHIPS) + core)

    def for_peers(act):
        pl.loop(0, CHIPS)(act)
        pl.loop(CHIPS + 1, BLOCK)(act)

    loads = [
        pltpu.make_async_copy(src, dst, local_sem.at[i])
        for i, (src, dst) in enumerate(
            [(tok_in, tok), (param_in, param), (ograd_in, ograd), (x_in, x),
             (win_in, win), (sout_in, sout), (wout_in, wout)]
        )
    ]
    for load in loads[:3]:
        load.start()

    barrier = pltpu.get_barrier_semaphore()

    def greet(n):
        _, _, device = peer(n)
        pl.semaphore_signal(barrier, inc=1, device_id=device, device_id_type=MESH)

    for_peers(greet)
    for device in (other, left, right):
        pl.semaphore_signal(barrier, inc=1, device_id=device, device_id_type=MESH)

    def softmax(logits):
        ex = jnp.exp(logits - jnp.max(logits, axis=0, keepdims=True))
        return ex / jnp.sum(ex, axis=0, keepdims=True)

    loads[0].wait()
    loads[1].wait()
    combine = softmax(matmul_t(param[...], tok[...]))
    loads[2].wait()
    whole = matmul(combine.astype(BF16), ograd[...])
    for i in range(cuts):
        part[i] = whole[:, i * LANES:(i + 1) * LANES]
        out_part[i] = part[i, pl.ds(1 - core, CHIPS, stride=2), :]
    for load in loads[3:]:
        load.start()
    tiles[...] = jnp.zeros_like(tiles)

    pl.semaphore_wait(barrier, BLOCK - 1 + 3)
    send_part = pltpu.make_async_remote_copy(
        out_part, pair_part, pair_send.at[0], pair_recv.at[0], device_id=other, device_id_type=MESH
    )
    send_part.start()
    send_part.wait_recv()
    for i in range(cuts):
        tiles[pl.ds(i, CHIPS, stride=PIECE), :] = part[i, pl.ds(core, CHIPS, stride=2), :] + pair_part[i]
    out_a[...] = tiles[pl.ds(0, CHIPS * PIECE), :].astype(BF16)

    def piece(ref, i):
        return ref.at[pl.ds(pl.multiple_of(i * PIECE, PIECE), PIECE)]

    all_but_one = pl.ds(0, (BLOCK - 1) * PIECE)

    def give_a(n):
        _, owner, device = peer(n)
        pltpu.make_async_remote_copy(
            piece(out_a, owner), piece(in_a, me), all_send.at[0], all_recv.at[0],
            device_id=device, device_id_type=MESH,
        ).start()

    for_peers(give_a)
    self_a = pltpu.make_async_copy(piece(out_a, chip), piece(in_a, me), all_self.at[0])
    self_a.start()

    mine = pl.ds(pl.multiple_of(CHIPS * core, 8), CHIPS)
    row = lax.broadcasted_iota(jnp.int32, (BLOCK, BLOCK), 0)
    col = lax.broadcasted_iota(jnp.int32, (BLOCK, BLOCK), 1)
    wanted = jnp.where(row < CHIPS, 2 * row, 2 * (row - CHIPS) + 1)
    perm = jnp.where(col == wanted, 1.0, 0.0).astype(BF16)
    param_p[...] = matmul(perm, param[...]).astype(BF16)
    logits = matmul_t(param_p[...], tok[...])
    combine = softmax(logits)
    col_max = jnp.max(logits, axis=1, keepdims=True)
    col_sum = jnp.sum(jnp.exp(logits - col_max), axis=1, keepdims=True)
    lse_own[...] = jnp.broadcast_to(col_max + jnp.log(col_sum), lse_own.shape)
    send_lse = pltpu.make_async_remote_copy(
        lse_own, lse_pair, pair_send.at[1], pair_recv.at[1], device_id=other, device_id_type=MESH
    )
    send_lse.start()
    loads[3].wait()
    for b in range(RING):
        lo = x[b * CHIPS:(b + 1) * CHIPS, :]
        hi = x[(RING + b) * CHIPS:(RING + b + 1) * CHIPS, :]
        xp[b * BLOCK:(b + 1) * BLOCK, :] = jnp.concatenate([lo, hi], axis=0)
    loads[4].wait()
    for i in range(xp.shape[0] // LANES):
        rows = slice(i * LANES, (i + 1) * LANES)
        act, rise = gelu_pair(matmul_t(xp[rows, :], win[...]))
        slope[rows, :] = rise
        act_t[:, rows] = act.T.astype(BF16)
    loads[5].wait()
    comb_grad = matmul_t(matmul(perm, sout[...]).astype(BF16), ograd[...])
    base[...] = combine * (comb_grad - jnp.sum(combine * comb_grad, axis=0, keepdims=True))
    send_lse.wait_recv()
    lse_a, lse_b = lse_own[...], lse_pair[...]
    top = jnp.maximum(lse_a, lse_b)
    lse = top + jnp.log(jnp.exp(lse_a - top) + jnp.exp(lse_b - top))
    disp[...] = jnp.exp(logits - lse)

    def rows_of(b):
        return pl.ds(pl.multiple_of(b * BLOCK, PIECE), BLOCK)

    pltpu.make_async_copy(in_a.at[all_but_one], in_a.at[all_but_one], all_recv.at[0]).wait()
    self_a.wait()
    tiles[...] = in_a[...].astype(F32)
    for i in range(cuts):
        grads[rows_of(y), i * LANES:(i + 1) * LANES] = tiles[pl.ds(i, BLOCK, stride=PIECE), :].astype(BF16)
    loads[6].wait()

    def work(blocks):
        g = [grads[rows_of(b), :] for b in blocks]
        s = [slope[rows_of(b), :] for b in blocks]
        g = g[0] if len(g) == 1 else jnp.concatenate(g, axis=0)
        s = s[0] if len(s) == 1 else jnp.concatenate(s, axis=0)
        pg = (matmul_t(g, wout[...]) * s).astype(BF16)
        total = matmul(pg, win[...])
        for i, b in enumerate(blocks):
            pgs[rows_of(b), :] = pg[i * BLOCK:(i + 1) * BLOCK, :]
            sums[rows_of(b), :] = total[i * BLOCK:(i + 1) * BLOCK, :]

    def at(offset):
        return (y + offset + RING) % RING

    sides = (right, left)
    ag = {}
    for s in range(4):
        for i in range(2):
            rows = rows_of(at(-s if i == 0 else s))
            for c in OPPOSITE[i] if s == 3 else range(4):
                ref = grads.at[rows, pl.ds(*PARTS[c])]
                ag[s, i, c] = pltpu.make_async_remote_copy(
                    ref, ref, ag_send.at[s, i, c], ag_recv.at[s, i, c],
                    device_id=sides[i], device_id_type=MESH,
                )
    for c in range(4):
        for i in range(2):
            ag[0, i, c].start()
    work([at(0)])
    for s in range(1, 4):
        for c in (0, 2, 1, 3):
            for i in range(2):
                ag[s - 1, i, c].wait_recv()
                if (s, i, c) in ag:
                    ag[s, i, c].start()
        work([at(-s), at(s)])
    for i in range(2):
        for c in OPPOSITE[i]:
            ag[3, i, c].wait_recv()
    work([at(4)])

    chunk = 2 * LANES

    def weight_out():
        for i in range(width // chunk):
            lanes = slice(i * chunk, (i + 1) * chunk)
            wout_out[:, lanes] = matmul(act_t[...], grads[:, lanes]).astype(BF16)

    def transpose_pg():
        for i in range(pgs.shape[0] // LANES):
            rows = slice(i * LANES, (i + 1) * LANES)
            pg_t[:, rows] = pgs[rows, :].astype(F32).T.astype(BF16)

    def weight_in(first, last):
        for i in range(first, last):
            lanes = slice(i * chunk, (i + 1) * chunk)
            win_out[:, lanes] = matmul(pg_t[...], xp[:, lanes]).astype(BF16)

    rs = {}

    def give_sum(s, i, c):
        dest = rows_of(at(4 - s if i == 0 else s - 4))
        lanes = pl.ds(*PARTS[c])
        term = sums[dest, lanes]
        if (s - 1, i, c) in rs:
            rs[s - 1, i, c].wait_recv()
            term = term + rs_in[s - 1, i, :, lanes].astype(F32)
        rs_out[s, i, :, lanes] = term.astype(BF16)
        rs[s, i, c] = pltpu.make_async_remote_copy(
            rs_out.at[s, i, :, lanes], rs_in.at[s, i, :, lanes], rs_send.at[s, i, c], rs_recv.at[s, i, c],
            device_id=sides[i], device_id_type=MESH,
        )
        rs[s, i, c].start()

    def give_sums(s, late):
        for k in range(2):
            for i in range(2):
                give_sum(s, i, OPPOSITE[i if late else 1 - i][k])

    give_sums(0, True)
    give_sums(1, False)
    weight_out()
    transpose_pg()
    give_sums(1, True)
    give_sums(2, False)
    weight_in(0, 2)
    give_sums(2, True)
    give_sums(3, False)
    weight_in(2, 5)
    give_sums(3, True)
    for i in range(2):
        for c in range(4):
            rs[3, i, c].wait_recv()

    total = (sums[rows_of(y), :] + rs_in[3, 0].astype(F32) + rs_in[3, 1].astype(F32)).astype(BF16).astype(F32)
    dot = jnp.sum(xp[rows_of(y), :].astype(F32) * total, axis=1, keepdims=True)
    dot_hi = dot.astype(BF16).astype(F32)
    for i in range(cuts):
        tiles[pl.ds(i, BLOCK, stride=PIECE), :] = total[:, i * LANES:(i + 1) * LANES]
    tiles[pl.ds(cuts, BLOCK, stride=PIECE), :] = jnp.broadcast_to(dot_hi, (BLOCK, LANES))
    tiles[pl.ds(cuts + 1, BLOCK, stride=PIECE), :] = jnp.broadcast_to(dot - dot_hi, (BLOCK, LANES))
    out_b[...] = tiles[...].astype(BF16)

    def give_b(n):
        t, _, device = peer(n)
        pltpu.make_async_remote_copy(
            piece(out_b, t), piece(in_b, me), all_send.at[1], all_recv.at[1],
            device_id=device, device_id_type=MESH,
        ).start()

    for_peers(give_b)
    self_b = pltpu.make_async_copy(piece(out_b, me), piece(in_b, me), all_self.at[1])
    self_b.start()
    pltpu.make_async_copy(in_b.at[all_but_one], in_b.at[all_but_one], all_recv.at[1]).wait()
    self_b.wait()

    tiles[...] = in_b[...].astype(F32)

    def both(i):
        v = tiles[pl.ds(i, BLOCK, stride=PIECE), :]
        return v[:CHIPS, :] + v[CHIPS:, :]

    for i in range(cuts):
        back[mine, i * LANES:(i + 1) * LANES] = both(i)
    back[mine, width:width + LANES] = both(cuts) + both(cuts + 1)
    send_back = pltpu.make_async_remote_copy(
        back.at[mine], back.at[mine], pair_send.at[2], pair_recv.at[2], device_id=other, device_id_type=MESH
    )
    send_back.start()
    send_back.wait_recv()

    send_part.wait_send()
    send_lse.wait_send()
    send_back.wait_send()
    for i in range(2):
        pltpu.make_async_copy(in_b.at[all_but_one], in_b.at[all_but_one], all_send.at[i]).wait()
    for copy in list(ag.values()) + list(rs.values()):
        copy.wait_send()


def finish(win_made, wout_made, tok, param_p, base, disp, back, tok_grad, win_grad, wout_grad, tok_out, sem):
    width = tok.shape[1]
    stores = [
        pltpu.make_async_copy(win_made, win_grad, sem.at[0]),
        pltpu.make_async_copy(wout_made, wout_grad, sem.at[1]),
    ]
    for store in stores:
        store.start()
    in_grad = back[:, :width].astype(BF16)
    disp_grad = matmul_t(in_grad, tok[...])
    logit_grad = base[...] + disp[...] * (disp_grad - back[:, width:width + LANES])
    left_t = jnp.concatenate([disp[...], logit_grad], axis=0).T.astype(BF16)
    half = width // 2
    for i in range(2):
        lanes = slice(i * half, (i + 1) * half)
        right_t = jnp.concatenate([in_grad[:, lanes], param_p[:, lanes]], axis=0)
        tok_out[:, lanes] = matmul(left_t, right_t).astype(BF16)
        store = pltpu.make_async_copy(tok_out.at[:, lanes], tok_grad.at[:, lanes], sem.at[2 + i])
        store.start()
        stores.append(store)
    for store in stores:
        store.wait()


def body(tokens, slot_param, out_grad, slot_outputs, slot_inputs, w_in, w_out):
    tok, ograd, sout = tokens[0], out_grad[0], slot_outputs[0]
    x = slot_inputs[:, 0]
    param = slot_param.T
    win, wout = w_in[0].T, w_out[0]
    images, width = x.shape
    hidden = wout.shape[0]
    slots = param.shape[0]
    tokens_here = tok.shape[0]
    vm = pltpu.VMEM
    dma = pltpu.SemaphoreType.DMA
    hbm = pl.BlockSpec(memory_space=pltpu.HBM)
    args = [pltpu.with_memory_space_constraint(v, pltpu.HBM) for v in (tok, param, ograd, sout, x, win, wout)]
    in_vmem = pl.BlockSpec(memory_space=pltpu.VMEM)
    made = pl.pallas_call(
        kernel,
        out_shape=(
            vm((hidden, width), BF16), vm((hidden, width), BF16), vm((tokens_here, width), BF16),
            vm((slots, width), BF16), vm((slots, LANES), F32), vm((slots, LANES), F32),
            vm((slots, width + LANES), F32),
        ),
        in_specs=[hbm] * 7,
        out_specs=(in_vmem,) * 7,
        scratch_shapes=[
            vm((slots, width), BF16), vm((tokens_here, width), BF16),
            vm((slots, width), BF16), vm((images, width), BF16), vm((hidden, width), BF16),
            vm((hidden, width), BF16),
            vm((images, width), BF16), vm((images, hidden), F32),
            vm((hidden, images), BF16), vm((images, width), BF16), vm((images, hidden), BF16),
            vm((hidden, images), BF16), vm((images, width), F32),
            vm((width // LANES, slots, LANES), F32), vm((width // LANES, CHIPS, LANES), F32),
            vm((slots, LANES), F32), vm((slots, LANES), F32),
            vm((BLOCK * PIECE, LANES), F32), vm((CHIPS * PIECE, LANES), BF16),
            vm((BLOCK * PIECE, LANES), BF16), vm((BLOCK * PIECE, LANES), BF16),
            vm((BLOCK * PIECE, LANES), BF16),
            vm((4, 2, BLOCK, width), BF16), vm((4, 2, BLOCK, width), BF16),
            vm((width // LANES, CHIPS, LANES), F32),
            dma((7,)), dma((3,)), dma((3,)), dma((2,)), dma((2,)), dma((2,)),
            dma((4, 2, 4)), dma((4, 2, 4)), dma((4, 2, 4)), dma((4, 2, 4)),
        ],
        compiler_params=pltpu.CompilerParams(
            collective_id=0, has_side_effects=True, vmem_limit_bytes=40 * 1024 * 1024
        ),
    )(*args)
    tok_grad, win_grad, wout_grad = pl.pallas_call(
        finish,
        out_shape=(
            jax.ShapeDtypeStruct((tokens_here, width), BF16),
            jax.ShapeDtypeStruct((hidden, width), BF16),
            jax.ShapeDtypeStruct((hidden, width), BF16),
        ),
        in_specs=[in_vmem] * 7,
        out_specs=(hbm,) * 3,
        scratch_shapes=[vm((tokens_here, width), BF16), dma((4,))],
        compiler_params=pltpu.CompilerParams(vmem_limit_bytes=32 * 1024 * 1024),
    )(*made)
    return tok_grad[None], win_grad.T[None], wout_grad[None]


def solution(mesh):
    placed = (
        P(("dp", "expert"), None, None),
        P(),
        P(("dp", "expert"), None, None),
        P(("dp", "expert"), None, None),
        P(None, "expert", None),
        P("expert", None, "dp"),
        P("expert", "dp", None),
    )
    return jax.shard_map(
        body,
        mesh=mesh,
        in_specs=placed,
        out_specs=(
            P(("dp", "expert"), None, None),
            P("expert", None, "dp"),
            P("expert", "dp", None),
        ),
        check_vma=False,
    )
```

time: 96.3 us -> 81.3 us (0.84)
  local copies, waits for them, and re-layouts: 9.74 us -> 0 us
  Pallas kernels: 85.5 us -> 80.5 us
    unnamed x17 -> x0, local copies, waits for them, and re-layouts: 9.74 us -> none
    pallas_call x1 -> x2, Pallas kernels: 85.5 us -> 80.5 us  [the longest x1 78.9 us: body(): pl.pallas_call(kernel, out_shape=(vm((hidden, width), BF16), vm((hidden,...]
where the time goes in v2:
time: 81.3 us; the launch traced here: 81.1 us
  Pallas kernels  80.5 us (99%)
    pallas_call x1, Pallas kernels, body(): pl.pallas_call(kernel, out_shape=(vm((hidden, width), BF16), vm((hidden,...  78.9 us

profile of v2, /device:TPU:1, one launch (start us, length us, event | category | flops | bytes accessed | tf_op | source)
XLA Modules:
  0.0 81.1 jit_solution(758491795896353346)
XLA Ops:
  0.6 78.9 %shard_map.94 = (bf16[320,1280]{1,0:T(8,128)(2,1)S(1)}, bf16[320,1280]{1,0:T(8,128)(2,1)S(1)}, bf16[128,1280]{1,0:T(8,128)(2,1)S(1)}, bf16[48,1280]{1,0:T(8,128)...) custom-call(bf16[128,1280]{1,0:T(8,128)(2,1)} %bitcast.17, ...), custom_call_target="tpu_custom_call" | custom-call | tf_op jit(solution)/shard_map/pallas_call | solution.py:351
  79.5 1.6 %shard_map.95 = (bf16[128,1280]{1,0:T(8,128)(2,1)}, bf16[320,1280]{1,0:T(8,128)(2,1)}, bf16[320,1280]{1,0:T(8,128)(2,1)}) custom-call(bf16[320,1280]{1,0:T(8,128)(2,1)S(1)} %get-tuple-element.13.win_made, bf16[320,1280]{1,0:T(8,128)(2,1)S(1)} %get-tuple-element.14.wout_made, bf16[128,1280]{1,0:T(8,128)(2,1)S(1)} %get-tuple-element.15.tok, ...), custom_call_target="tpu_custom_call" | custom-call | tf_op jit(solution)/shard_map/pallas_call | solution.py:381

commit v3 on v2

--- a/solution.py
+++ b/solution.py
@@ -11,9 +11,10 @@
 
 RING = 8
 HALVES = 2
+ROW = 4
 CHIPS = 24
 BLOCK = HALVES * CHIPS
-PIECE = 16
+ALIGN = 16
 LANES = 128
 PARTS = ((0, 384), (384, 256), (640, 384), (1024, 256))
 OPPOSITE = ((0, 1), (2, 3))
@@ -39,7 +40,7 @@
     param, ograd, sout, x, win, wout,
     xp, slope, act_t, grads, pgs, pg_t, sums,
     part, pair_part, lse_own, lse_pair,
-    tiles, out_a, in_a, out_b, in_b,
+    out_a, in_a, out_b, in_b,
     rs_out, rs_in, out_part,
     local_sem, pair_send, pair_recv, all_send, all_recv, all_self,
     ag_send, ag_recv, rs_send, rs_recv,
@@ -55,13 +56,18 @@
     right = (zh * RING + (y + 1) % RING, e)
     left = (zh * RING + (y + RING - 1) % RING, e)
 
+    z, line = zh * (CHIPS // ROW) + chip // ROW, chip % ROW
+    length = BLOCK // ROW
+
     def peer(n):
-        t = (me + CHIPS + n) % BLOCK
+        step = n // ROW
+        far = (z + length // 2 + (step + 1) // 2 * (1 - 2 * (step % 2))) % length
+        t = far * ROW + (line + n) % ROW
         return t, t % CHIPS, ((t // CHIPS) * RING + y, 2 * (t % CHIPS) + core)
 
     def for_peers(act):
-        pl.loop(0, CHIPS)(act)
-        pl.loop(CHIPS + 1, BLOCK)(act)
+        pl.loop(0, BLOCK - ROW)(act)
+        pl.loop(BLOCK - ROW + 1, BLOCK)(act)
 
     loads = [
         pltpu.make_async_copy(src, dst, local_sem.at[i])
@@ -97,7 +103,6 @@
         out_part[i] = part[i, pl.ds(1 - core, CHIPS, stride=2), :]
     for load in loads[3:]:
         load.start()
-    tiles[...] = jnp.zeros_like(tiles)
 
     pl.semaphore_wait(barrier, BLOCK - 1 + 3)
     send_part = pltpu.make_async_remote_copy(
@@ -105,24 +110,21 @@
     )
     send_part.start()
     send_part.wait_recv()
-    for i in range(cuts):
-        tiles[pl.ds(i, CHIPS, stride=PIECE), :] = part[i, pl.ds(core, CHIPS, stride=2), :] + pair_part[i]
-    out_a[...] = tiles[pl.ds(0, CHIPS * PIECE), :].astype(BF16)
-
-    def piece(ref, i):
-        return ref.at[pl.ds(pl.multiple_of(i * PIECE, PIECE), PIECE)]
-
-    all_but_one = pl.ds(0, (BLOCK - 1) * PIECE)
+    slot_sum = [part[i, pl.ds(core, CHIPS, stride=2), :] + pair_part[i] for i in range(cuts)]
+    for i in range(cuts // 2):
+        out_a[:, i] = jnp.stack(slot_sum[2 * i:2 * i + 2], axis=1).astype(BF16)
+
+    all_but_one = pl.ds(0, BLOCK - 1)
 
     def give_a(n):
         _, owner, device = peer(n)
         pltpu.make_async_remote_copy(
-            piece(out_a, owner), piece(in_a, me), all_send.at[0], all_recv.at[0],
+            out_a.at[owner], in_a.at[me], all_send.at[0], all_recv.at[0],
             device_id=device, device_id_type=MESH,
         ).start()
 
     for_peers(give_a)
-    self_a = pltpu.make_async_copy(piece(out_a, chip), piece(in_a, me), all_self.at[0])
+    self_a = pltpu.make_async_copy(out_a.at[chip], in_a.at[me], all_self.at[0])
     self_a.start()
 
     mine = pl.ds(pl.multiple_of(CHIPS * core, 8), CHIPS)
@@ -161,13 +163,12 @@
     disp[...] = jnp.exp(logits - lse)
 
     def rows_of(b):
-        return pl.ds(pl.multiple_of(b * BLOCK, PIECE), BLOCK)
+        return pl.ds(pl.multiple_of(b * BLOCK, ALIGN), BLOCK)
 
     pltpu.make_async_copy(in_a.at[all_but_one], in_a.at[all_but_one], all_recv.at[0]).wait()
     self_a.wait()
-    tiles[...] = in_a[...].astype(F32)
     for i in range(cuts):
-        grads[rows_of(y), i * LANES:(i + 1) * LANES] = tiles[pl.ds(i, BLOCK, stride=PIECE), :].astype(BF16)
+        grads[rows_of(y), i * LANES:(i + 1) * LANES] = in_a[:, i // 2].astype(F32)[:, i % 2].astype(BF16)
     loads[6].wait()
 
     def work(blocks):
@@ -209,7 +210,9 @@
     for i in range(2):
         for c in OPPOSITE[i]:
             ag[3, i, c].wait_recv()
-    work([at(4)])
+    far = rows_of(at(4))
+    far_grad = (matmul_t(grads[far, :], wout[...]) * slope[far, :]).astype(BF16)
+    pgs[far, :] = far_grad
 
     chunk = 2 * LANES
 
@@ -233,7 +236,7 @@
     def give_sum(s, i, c):
         dest = rows_of(at(4 - s if i == 0 else s - 4))
         lanes = pl.ds(*PARTS[c])
-        term = sums[dest, lanes]
+        term = sums[dest, lanes] if s else matmul(far_grad, win[:, lanes])
         if (s - 1, i, c) in rs:
             rs[s - 1, i, c].wait_recv()
             term = term + rs_in[s - 1, i, :, lanes].astype(F32)
@@ -267,34 +270,31 @@
     total = (sums[rows_of(y), :] + rs_in[3, 0].astype(F32) + rs_in[3, 1].astype(F32)).astype(BF16).astype(F32)
     dot = jnp.sum(xp[rows_of(y), :].astype(F32) * total, axis=1, keepdims=True)
     dot_hi = dot.astype(BF16).astype(F32)
-    for i in range(cuts):
-        tiles[pl.ds(i, BLOCK, stride=PIECE), :] = total[:, i * LANES:(i + 1) * LANES]
-    tiles[pl.ds(cuts, BLOCK, stride=PIECE), :] = jnp.broadcast_to(dot_hi, (BLOCK, LANES))
-    tiles[pl.ds(cuts + 1, BLOCK, stride=PIECE), :] = jnp.broadcast_to(dot - dot_hi, (BLOCK, LANES))
-    out_b[...] = tiles[...].astype(BF16)
+    columns = [total[:, i * LANES:(i + 1) * LANES] for i in range(cuts)]
+    columns += [jnp.broadcast_to(v, (BLOCK, LANES)) for v in (dot_hi, dot - dot_hi)]
+    for i in range(cuts // 2 + 1):
+        out_b[:, i] = jnp.stack(columns[2 * i:2 * i + 2], axis=1).astype(BF16)
 
     def give_b(n):
         t, _, device = peer(n)
         pltpu.make_async_remote_copy(
-            piece(out_b, t), piece(in_b, me), all_send.at[1], all_recv.at[1],
+            out_b.at[t], in_b.at[me], all_send.at[1], all_recv.at[1],
             device_id=device, device_id_type=MESH,
         ).start()
 
     for_peers(give_b)
-    self_b = pltpu.make_async_copy(piece(out_b, me), piece(in_b, me), all_self.at[1])
+    self_b = pltpu.make_async_copy(out_b.at[me], in_b.at[me], all_self.at[1])
     self_b.start()
     pltpu.make_async_copy(in_b.at[all_but_one], in_b.at[all_but_one], all_recv.at[1]).wait()
     self_b.wait()
 
-    tiles[...] = in_b[...].astype(F32)
-
-    def both(i):
-        v = tiles[pl.ds(i, BLOCK, stride=PIECE), :]
-        return v[:CHIPS, :] + v[CHIPS:, :]
-
-    for i in range(cuts):
-        back[mine, i * LANES:(i + 1) * LANES] = both(i)
-    back[mine, width:width + LANES] = both(cuts) + both(cuts + 1)
+    for i in range(cuts // 2 + 1):
+        v = in_b[:CHIPS, i].astype(F32) + in_b[CHIPS:, i].astype(F32)
+        if i < cuts // 2:
+            for k in range(2):
+                back[mine, (2 * i + k) * LANES:(2 * i + k + 1) * LANES] = v[:, k]
+        else:
+            back[mine, width:width + LANES] = v[:, 0] + v[:, 1]
     send_back = pltpu.make_async_remote_copy(
         back.at[mine], back.at[mine], pair_send.at[2], pair_recv.at[2], device_id=other, device_id_type=MESH
     )
@@ -304,8 +304,8 @@
     send_part.wait_send()
     send_lse.wait_send()
     send_back.wait_send()
-    for i in range(2):
-        pltpu.make_async_copy(in_b.at[all_but_one], in_b.at[all_but_one], all_send.at[i]).wait()
+    for i, held in enumerate((in_a, in_b)):
+        pltpu.make_async_copy(held.at[all_but_one], held.at[all_but_one], all_send.at[i]).wait()
     for copy in list(ag.values()) + list(rs.values()):
         copy.wait_send()
 
@@ -343,6 +343,7 @@
     hidden = wout.shape[0]
     slots = param.shape[0]
     tokens_here = tok.shape[0]
+    pieces = width // (2 * LANES)
     vm = pltpu.VMEM
     dma = pltpu.SemaphoreType.DMA
     hbm = pl.BlockSpec(memory_space=pltpu.HBM)
@@ -366,9 +367,8 @@
             vm((hidden, images), BF16), vm((images, width), F32),
             vm((width // LANES, slots, LANES), F32), vm((width // LANES, CHIPS, LANES), F32),
             vm((slots, LANES), F32), vm((slots, LANES), F32),
-            vm((BLOCK * PIECE, LANES), F32), vm((CHIPS * PIECE, LANES), BF16),
-            vm((BLOCK * PIECE, LANES), BF16), vm((BLOCK * PIECE, LANES), BF16),
-            vm((BLOCK * PIECE, LANES), BF16),
+            vm((CHIPS, pieces, 2, LANES), BF16), vm((BLOCK, pieces, 2, LANES), BF16),
+            vm((BLOCK, pieces + 1, 2, LANES), BF16), vm((BLOCK, pieces + 1, 2, LANES), BF16),
             vm((4, 2, BLOCK, width), BF16), vm((4, 2, BLOCK, width), BF16),
             vm((width // LANES, CHIPS, LANES), F32),
             dma((7,)), dma((3,)), dma((3,)), dma((2,)), dma((2,)), dma((2,)),

time: 81.3 us -> 73.9 us (0.909)
  Pallas kernels: 80.5 us -> 73.2 us
    pallas_call x1, Pallas kernels: 78.9 us -> 71.6 us  [body(): pl.pallas_call(kernel, out_shape=(vm((hidden, width), BF16), vm((hidden,...]
where the time goes in v3:
time: 73.9 us; the launch traced here: 73.8 us
  Pallas kernels  73.2 us (99%)
    pallas_call x1, Pallas kernels, body(): pl.pallas_call(kernel, out_shape=(vm((hidden, width), BF16), vm((hidden,...  71.6 us
    pallas_call x1, Pallas kernels, body(): pl.pallas_call(finish, out_shape=(jax.ShapeDtypeStruct((tokens_here, widt...  1.59 us

profile of v3, /device:TPU:1, one launch (start us, length us, event | category | flops | bytes accessed | tf_op | source)
XLA Modules:
  0.0 73.8 jit_solution(14324932853301547360)
XLA Ops:
  0.6 71.6 %shard_map.94 = (bf16[320,1280]{1,0:T(8,128)(2,1)S(1)}, bf16[320,1280]{1,0:T(8,128)(2,1)S(1)}, bf16[128,1280]{1,0:T(8,128)(2,1)S(1)}, bf16[48,1280]{1,0:T(8,128)...) custom-call(bf16[128,1280]{1,0:T(8,128)(2,1)} %bitcast.17, ...), custom_call_target="tpu_custom_call" | custom-call | tf_op jit(solution)/shard_map/pallas_call | solution.py:352
  72.2 1.6 %shard_map.95 = (bf16[128,1280]{1,0:T(8,128)(2,1)}, bf16[320,1280]{1,0:T(8,128)(2,1)}, bf16[320,1280]{1,0:T(8,128)(2,1)}) custom-call(bf16[320,1280]{1,0:T(8,128)(2,1)S(1)} %get-tuple-element.13.win_made, bf16[320,1280]{1,0:T(8,128)(2,1)S(1)} %get-tuple-element.14.wout_made, bf16[128,1280]{1,0:T(8,128)(2,1)S(1)} %get-tuple-element.15.tok, ...), custom_call_target="tpu_custom_call" | custom-call | tf_op jit(solution)/shard_map/pallas_call | solution.py:381

commit v4 on v3

--- a/solution.py
+++ b/solution.py
@@ -16,8 +16,7 @@
 BLOCK = HALVES * CHIPS
 ALIGN = 16
 LANES = 128
-PARTS = ((0, 384), (384, 256), (640, 384), (1024, 256))
-OPPOSITE = ((0, 1), (2, 3))
+ROW_PARTS = BLOCK // ALIGN
 
 
 def matmul(a, b):
@@ -171,48 +170,66 @@
         grads[rows_of(y), i * LANES:(i + 1) * LANES] = in_a[:, i // 2].astype(F32)[:, i % 2].astype(BF16)
     loads[6].wait()
 
-    def work(blocks):
-        g = [grads[rows_of(b), :] for b in blocks]
-        s = [slope[rows_of(b), :] for b in blocks]
-        g = g[0] if len(g) == 1 else jnp.concatenate(g, axis=0)
-        s = s[0] if len(s) == 1 else jnp.concatenate(s, axis=0)
-        pg = (matmul_t(g, wout[...]) * s).astype(BF16)
-        total = matmul(pg, win[...])
-        for i, b in enumerate(blocks):
-            pgs[rows_of(b), :] = pg[i * BLOCK:(i + 1) * BLOCK, :]
-            sums[rows_of(b), :] = total[i * BLOCK:(i + 1) * BLOCK, :]
-
     def at(offset):
         return (y + offset + RING) % RING
 
     sides = (right, left)
+    half = width // 2
+    sides_lanes = (pl.ds(0, half), pl.ds(half, half))
+
+    def rows_part(b, r):
+        return pl.ds(pl.multiple_of(b * BLOCK + r * ALIGN, ALIGN), ALIGN)
+
+    every = [(r, i if ahead else 1 - i, i) for ahead in (True, False) for r in range(ROW_PARTS) for i in range(2)]
     ag = {}
     for s in range(4):
-        for i in range(2):
-            rows = rows_of(at(-s if i == 0 else s))
-            for c in OPPOSITE[i] if s == 3 else range(4):
-                ref = grads.at[rows, pl.ds(*PARTS[c])]
-                ag[s, i, c] = pltpu.make_async_remote_copy(
-                    ref, ref, ag_send.at[s, i, c], ag_recv.at[s, i, c],
+        for r, h, i in every:
+            if s < 3 or h == i:
+                ref = grads.at[rows_part(at(-s if i == 0 else s), r), sides_lanes[h]]
+                ag[s, r, h, i] = pltpu.make_async_remote_copy(
+                    ref, ref, ag_send.at[s, i, r, h], ag_recv.at[s, i, r, h],
                     device_id=sides[i], device_id_type=MESH,
                 )
-    for c in range(4):
-        for i in range(2):
-            ag[0, i, c].start()
-    work([at(0)])
+    for r, h, i in every:
+        ag[0, r, h, i].start()
     for s in range(1, 4):
-        for c in (0, 2, 1, 3):
-            for i in range(2):
-                ag[s - 1, i, c].wait_recv()
-                if (s, i, c) in ag:
-                    ag[s, i, c].start()
-        work([at(-s), at(s)])
-    for i in range(2):
-        for c in OPPOSITE[i]:
-            ag[3, i, c].wait_recv()
+        for r, h, i in every:
+            ag[s - 1, r, h, i].wait_recv()
+            if (s, r, h, i) in ag:
+                ag[s, r, h, i].start()
+    for r, h, i in every:
+        if h == i:
+            ag[3, r, h, i].wait_recv()
+
     far = rows_of(at(4))
     far_grad = (matmul_t(grads[far, :], wout[...]) * slope[far, :]).astype(BF16)
-    pgs[far, :] = far_grad
+    rs = {}
+
+    def give_sum(s, r, h, i, term):
+        rows = pl.ds(r * ALIGN, ALIGN)
+        rs_out[s, i, rows, sides_lanes[h]] = term.astype(BF16)
+        rs[s, r, h, i] = pltpu.make_async_remote_copy(
+            rs_out.at[s, i, rows, sides_lanes[h]], rs_in.at[s, i, rows, sides_lanes[h]],
+            rs_send.at[s, i, r, h], rs_recv.at[s, i, r, h], device_id=sides[i], device_id_type=MESH,
+        )
+        rs[s, r, h, i].start()
+
+    def give_sums(s, late):
+        for r, h, i in every:
+            if (h == i) == late:
+                term = sums[rows_part(at(4 - s if i == 0 else s - 4), r), sides_lanes[h]]
+                if (s - 1, r, h, i) in rs:
+                    rs[s - 1, r, h, i].wait_recv()
+                    term = term + rs_in[s - 1, i, r * ALIGN:(r + 1) * ALIGN, sides_lanes[h]].astype(F32)
+                give_sum(s, r, h, i, term)
+
+    for i in range(2):
+        term = matmul(far_grad, win[:, sides_lanes[i]])
+        for r in range(ROW_PARTS):
+            give_sum(0, r, i, i, term[r * ALIGN:(r + 1) * ALIGN, :])
+
+    pgs[...] = (matmul_t(grads[...], wout[...]) * slope[...]).astype(BF16)
+    sums[...] = matmul(pgs[...], win[...])
 
     chunk = 2 * LANES
 
@@ -226,46 +243,22 @@
             rows = slice(i * LANES, (i + 1) * LANES)
             pg_t[:, rows] = pgs[rows, :].astype(F32).T.astype(BF16)
 
-    def weight_in(first, last):
-        for i in range(first, last):
+    def weight_in():
+        for i in range(width // chunk):
             lanes = slice(i * chunk, (i + 1) * chunk)
             win_out[:, lanes] = matmul(pg_t[...], xp[:, lanes]).astype(BF16)
 
-    rs = {}
-
-    def give_sum(s, i, c):
-        dest = rows_of(at(4 - s if i == 0 else s - 4))
-        lanes = pl.ds(*PARTS[c])
-        term = sums[dest, lanes] if s else matmul(far_grad, win[:, lanes])
-        if (s - 1, i, c) in rs:
-            rs[s - 1, i, c].wait_recv()
-            term = term + rs_in[s - 1, i, :, lanes].astype(F32)
-        rs_out[s, i, :, lanes] = term.astype(BF16)
-        rs[s, i, c] = pltpu.make_async_remote_copy(
-            rs_out.at[s, i, :, lanes], rs_in.at[s, i, :, lanes], rs_send.at[s, i, c], rs_recv.at[s, i, c],
-            device_id=sides[i], device_id_type=MESH,
-        )
-        rs[s, i, c].start()
-
-    def give_sums(s, late):
-        for k in range(2):
-            for i in range(2):
-                give_sum(s, i, OPPOSITE[i if late else 1 - i][k])
-
-    give_sums(0, True)
     give_sums(1, False)
     weight_out()
     transpose_pg()
     give_sums(1, True)
     give_sums(2, False)
-    weight_in(0, 2)
     give_sums(2, True)
     give_sums(3, False)
-    weight_in(2, 5)
     give_sums(3, True)
-    for i in range(2):
-        for c in range(4):
-            rs[3, i, c].wait_recv()
+    weight_in()
+    for r, h, i in every:
+        rs[3, r, h, i].wait_recv()
 
     total = (sums[rows_of(y), :] + rs_in[3, 0].astype(F32) + rs_in[3, 1].astype(F32)).astype(BF16).astype(F32)
     dot = jnp.sum(xp[rows_of(y), :].astype(F32) * total, axis=1, keepdims=True)
@@ -372,7 +365,8 @@
             vm((4, 2, BLOCK, width), BF16), vm((4, 2, BLOCK, width), BF16),
             vm((width // LANES, CHIPS, LANES), F32),
             dma((7,)), dma((3,)), dma((3,)), dma((2,)), dma((2,)), dma((2,)),
-            dma((4, 2, 4)), dma((4, 2, 4)), dma((4, 2, 4)), dma((4, 2, 4)),
+            dma((4, 2, ROW_PARTS, 2)), dma((4, 2, ROW_PARTS, 2)), dma((4, 2, ROW_PARTS, 2)),
+            dma((4, 2, ROW_PARTS, 2)),
         ],
         compiler_params=pltpu.CompilerParams(
             collective_id=0, has_side_effects=True, vmem_limit_bytes=40 * 1024 * 1024

time: 73.9 us -> 72.4 us (0.980)
  Pallas kernels: 73.2 us -> 71.7 us
    pallas_call x1, Pallas kernels: 71.6 us -> 70.1 us  [body(): pl.pallas_call(kernel, out_shape=(vm((hidden, width), BF16), vm((hidden,...]
where the time goes in v4:
time: 72.4 us; the launch traced here: 72.3 us
  Pallas kernels  71.7 us (99%)
    pallas_call x1, Pallas kernels, body(): pl.pallas_call(kernel, out_shape=(vm((hidden, width), BF16), vm((hidden,...  70.1 us
    pallas_call x1, Pallas kernels, body(): pl.pallas_call(finish, out_shape=(jax.ShapeDtypeStruct((tokens_here, widt...  1.59 us

profile of v4, /device:TPU:1, one launch (start us, length us, event | category | flops | bytes accessed | tf_op | source)
XLA Modules:
  0.0 72.3 jit_solution(4735823492261028942)
XLA Ops:
  0.6 70.1 %shard_map.94 = (bf16[320,1280]{1,0:T(8,128)(2,1)S(1)}, bf16[320,1280]{1,0:T(8,128)(2,1)S(1)}, bf16[128,1280]{1,0:T(8,128)(2,1)S(1)}, bf16[48,1280]{1,0:T(8,128)...) custom-call(bf16[128,1280]{1,0:T(8,128)(2,1)} %bitcast.17, ...), custom_call_target="tpu_custom_call" | custom-call | tf_op jit(solution)/shard_map/pallas_call | solution.py:345
  70.7 1.6 %shard_map.95 = (bf16[128,1280]{1,0:T(8,128)(2,1)}, bf16[320,1280]{1,0:T(8,128)(2,1)}, bf16[320,1280]{1,0:T(8,128)(2,1)}) custom-call(bf16[320,1280]{1,0:T(8,128)(2,1)S(1)} %get-tuple-element.13.win_made, bf16[320,1280]{1,0:T(8,128)(2,1)S(1)} %get-tuple-element.14.wout_made, bf16[128,1280]{1,0:T(8,128)(2,1)S(1)} %get-tuple-element.15.tok, ...), custom_call_target="tpu_custom_call" | custom-call | tf_op jit(solution)/shard_map/pallas_call | solution.py:375

commit v5 on v4

--- a/solution.py
+++ b/solution.py
@@ -54,6 +54,8 @@
     other = (d, e + 1 - 2 * core)
     right = (zh * RING + (y + 1) % RING, e)
     left = (zh * RING + (y + RING - 1) % RING, e)
+    right2 = (zh * RING + (y + 2) % RING, e)
+    left2 = (zh * RING + (y + RING - 2) % RING, e)
 
     z, line = zh * (CHIPS // ROW) + chip // ROW, chip % ROW
     length = BLOCK // ROW
@@ -85,7 +87,7 @@
         pl.semaphore_signal(barrier, inc=1, device_id=device, device_id_type=MESH)
 
     for_peers(greet)
-    for device in (other, left, right):
+    for device in (other, left, right, left2, right2):
         pl.semaphore_signal(barrier, inc=1, device_id=device, device_id_type=MESH)
 
     def softmax(logits):
@@ -103,7 +105,7 @@
     for load in loads[3:]:
         load.start()
 
-    pl.semaphore_wait(barrier, BLOCK - 1 + 3)
+    pl.semaphore_wait(barrier, BLOCK - 1 + 5)
     send_part = pltpu.make_async_remote_copy(
         out_part, pair_part, pair_send.at[0], pair_recv.at[0], device_id=other, device_id_type=MESH
     )
@@ -173,7 +175,7 @@
     def at(offset):
         return (y + offset + RING) % RING
 
-    sides = (right, left)
+    sides, skips = (right, left), (right2, left2)
     half = width // 2
     sides_lanes = (pl.ds(0, half), pl.ds(half, half))
 
@@ -185,21 +187,24 @@
     for s in range(4):
         for r, h, i in every:
             if s < 3 or h == i:
-                ref = grads.at[rows_part(at(-s if i == 0 else s), r), sides_lanes[h]]
+                away = min(s, 2)
+                ref = grads.at[rows_part(at(-away if i == 0 else away), r), sides_lanes[h]]
                 ag[s, r, h, i] = pltpu.make_async_remote_copy(
                     ref, ref, ag_send.at[s, i, r, h], ag_recv.at[s, i, r, h],
-                    device_id=sides[i], device_id_type=MESH,
+                    device_id=(skips if s == 3 else sides)[i], device_id_type=MESH,
                 )
     for r, h, i in every:
         ag[0, r, h, i].start()
-    for s in range(1, 4):
+    for s in range(1, 3):
         for r, h, i in every:
             ag[s - 1, r, h, i].wait_recv()
-            if (s, r, h, i) in ag:
-                ag[s, r, h, i].start()
-    for r, h, i in every:
-        if h == i:
-            ag[3, r, h, i].wait_recv()
+            if s == 2 and h == i:
+                ag[3, r, h, i].start()
+            ag[s, r, h, i].start()
+    for s in range(2, 4):
+        for r, h, i in every:
+            if s == 2 or h == i:
+                ag[s, r, h, i].wait_recv()
 
     far = rows_of(at(4))
     far_grad = (matmul_t(grads[far, :], wout[...]) * slope[far, :]).astype(BF16)

time: 72.4 us -> 72.2 us (level)
  no operation moved by 1% of the time
where the time goes in v5:
time: 72.2 us; the launch traced here: 72.1 us
  Pallas kernels  71.4 us (99%)
    pallas_call x1, Pallas kernels, body(): pl.pallas_call(kernel, out_shape=(vm((hidden, width), BF16), vm((hidden,...  69.8 us
    pallas_call x1, Pallas kernels, body(): pl.pallas_call(finish, out_shape=(jax.ShapeDtypeStruct((tokens_here, widt...  1.59 us

profile of v5, /device:TPU:1, one launch (start us, length us, event | category | flops | bytes accessed | tf_op | source)
XLA Modules:
  0.0 72.1 jit_solution(14433960475129621959)
XLA Ops:
  0.6 69.8 %shard_map.94 = (bf16[320,1280]{1,0:T(8,128)(2,1)S(1)}, bf16[320,1280]{1,0:T(8,128)(2,1)S(1)}, bf16[128,1280]{1,0:T(8,128)(2,1)S(1)}, bf16[48,1280]{1,0:T(8,128)...) custom-call(bf16[128,1280]{1,0:T(8,128)(2,1)} %bitcast.17, ...), custom_call_target="tpu_custom_call" | custom-call | tf_op jit(solution)/shard_map/pallas_call | solution.py:350
  70.5 1.6 %shard_map.95 = (bf16[128,1280]{1,0:T(8,128)(2,1)}, bf16[320,1280]{1,0:T(8,128)(2,1)}, bf16[320,1280]{1,0:T(8,128)(2,1)}) custom-call(bf16[320,1280]{1,0:T(8,128)(2,1)S(1)} %get-tuple-element.13.win_made, bf16[320,1280]{1,0:T(8,128)(2,1)S(1)} %get-tuple-element.14.wout_made, bf16[128,1280]{1,0:T(8,128)(2,1)S(1)} %get-tuple-element.15.tok, ...), custom_call_target="tpu_custom_call" | custom-call | tf_op jit(solution)/shard_map/pallas_call | solution.py:380

commit v6 on v5

--- a/solution.py
+++ b/solution.py
@@ -179,8 +179,11 @@
     half = width // 2
     sides_lanes = (pl.ds(0, half), pl.ds(half, half))
 
+    def place(r):
+        return zh * r + (1 - zh) * (ROW_PARTS - 1 - r)
+
     def rows_part(b, r):
-        return pl.ds(pl.multiple_of(b * BLOCK + r * ALIGN, ALIGN), ALIGN)
+        return pl.ds(pl.multiple_of(b * BLOCK + place(r) * ALIGN, ALIGN), ALIGN)
 
     every = [(r, i if ahead else 1 - i, i) for ahead in (True, False) for r in range(ROW_PARTS) for i in range(2)]
     ag = {}
@@ -229,9 +232,9 @@
                 give_sum(s, r, h, i, term)
 
     for i in range(2):
-        term = matmul(far_grad, win[:, sides_lanes[i]])
+        sums[far, sides_lanes[i]] = matmul(far_grad, win[:, sides_lanes[i]])
         for r in range(ROW_PARTS):
-            give_sum(0, r, i, i, term[r * ALIGN:(r + 1) * ALIGN, :])
+            give_sum(0, r, i, i, sums[rows_part(at(4), r), sides_lanes[i]])
 
     pgs[...] = (matmul_t(grads[...], wout[...]) * slope[...]).astype(BF16)
     sums[...] = matmul(pgs[...], win[...])
@@ -262,25 +265,32 @@
     give_sums(3, False)
     give_sums(3, True)
     weight_in()
-    for r, h, i in every:
-        rs[3, r, h, i].wait_recv()
-
-    total = (sums[rows_of(y), :] + rs_in[3, 0].astype(F32) + rs_in[3, 1].astype(F32)).astype(BF16).astype(F32)
-    dot = jnp.sum(xp[rows_of(y), :].astype(F32) * total, axis=1, keepdims=True)
-    dot_hi = dot.astype(BF16).astype(F32)
-    columns = [total[:, i * LANES:(i + 1) * LANES] for i in range(cuts)]
-    columns += [jnp.broadcast_to(v, (BLOCK, LANES)) for v in (dot_hi, dot - dot_hi)]
-    for i in range(cuts // 2 + 1):
-        out_b[:, i] = jnp.stack(columns[2 * i:2 * i + 2], axis=1).astype(BF16)
-
-    def give_b(n):
-        t, _, device = peer(n)
-        pltpu.make_async_remote_copy(
-            out_b.at[t], in_b.at[me], all_send.at[1], all_recv.at[1],
-            device_id=device, device_id_type=MESH,
-        ).start()
-
-    for_peers(give_b)
+    for r in range(ROW_PARTS):
+        for h in range(2):
+            for i in range(2):
+                rs[3, r, h, i].wait_recv()
+        got = slice(r * ALIGN, (r + 1) * ALIGN)
+        total = sums[rows_part(y, r), :] + rs_in[3, 0, got, :].astype(F32) + rs_in[3, 1, got, :].astype(F32)
+        total = total.astype(BF16).astype(F32)
+        dot = jnp.sum(xp[rows_part(y, r), :].astype(F32) * total, axis=1, keepdims=True)
+        dot_hi = dot.astype(BF16).astype(F32)
+        columns = [total[:, i * LANES:(i + 1) * LANES] for i in range(cuts)]
+        columns += [jnp.broadcast_to(v, (ALIGN, LANES)) for v in (dot_hi, dot - dot_hi)]
+        first = place(r) * ALIGN
+        for i in range(cuts // 2 + 1):
+            out_b[pl.ds(first, ALIGN), i] = jnp.stack(columns[2 * i:2 * i + 2], axis=1).astype(BF16)
+
+        @pl.loop(0, ALIGN)
+        def _(n):
+            t = first + (n + chip) % ALIGN
+
+            @pl.when(t != me)
+            def _():
+                pltpu.make_async_remote_copy(
+                    out_b.at[t], in_b.at[me], all_send.at[1], all_recv.at[1],
+                    device_id=((t // CHIPS) * RING + y, 2 * (t % CHIPS) + core), device_id_type=MESH,
+                ).start()
+
     self_b = pltpu.make_async_copy(out_b.at[me], in_b.at[me], all_self.at[1])
     self_b.start()
     pltpu.make_async_copy(in_b.at[all_but_one], in_b.at[all_but_one], all_recv.at[1]).wait()

time: 72.2 us -> 72.2 us (level)
  no operation moved by 1% of the time
where the time goes in v6:
time: 72.2 us; the launch traced here: 72.1 us
  Pallas kernels  71.4 us (99%)
    pallas_call x1, Pallas kernels, body(): pl.pallas_call(kernel, out_shape=(vm((hidden, width), BF16), vm((hidden,...  69.8 us
    pallas_call x1, Pallas kernels, body(): pl.pallas_call(finish, out_shape=(jax.ShapeDtypeStruct((tokens_here, widt...  1.59 us

profile of v6, /device:TPU:1, one launch (start us, length us, event | category | flops | bytes accessed | tf_op | source)
XLA Modules:
  0.0 72.1 jit_solution(9564279548214632463)
XLA Ops:
  0.6 69.8 %shard_map.94 = (bf16[320,1280]{1,0:T(8,128)(2,1)S(1)}, bf16[320,1280]{1,0:T(8,128)(2,1)S(1)}, bf16[128,1280]{1,0:T(8,128)(2,1)S(1)}, bf16[48,1280]{1,0:T(8,128)...) custom-call(bf16[128,1280]{1,0:T(8,128)(2,1)} %bitcast.17, ...), custom_call_target="tpu_custom_call" | custom-call | tf_op jit(solution)/shard_map/pallas_call | solution.py:360
  70.5 1.6 %shard_map.95 = (bf16[128,1280]{1,0:T(8,128)(2,1)}, bf16[320,1280]{1,0:T(8,128)(2,1)}, bf16[320,1280]{1,0:T(8,128)(2,1)}) custom-call(bf16[320,1280]{1,0:T(8,128)(2,1)S(1)} %get-tuple-element.13.win_made, bf16[320,1280]{1,0:T(8,128)(2,1)S(1)} %get-tuple-element.14.wout_made, bf16[128,1280]{1,0:T(8,128)(2,1)S(1)} %get-tuple-element.15.tok, ...), custom_call_target="tpu_custom_call" | custom-call | tf_op jit(solution)/shard_map/pallas_call | solution.py:390
